TPU v7x, 32 devices: a whole 2x2x4 slice. The times are simulated.
32 devices in a mesh: ex: 8 (over y, x, core), feat: 4 (over z).
Axes of the slice: x: 2, y: 2, z: 4, core: 2. Of those that a mesh axis runs over, the one named last changes fastest.
Arguments:
- train_grads: bfloat16 [8192, 16384], P('ex', 'feat'), may hold values from -200 to 200
- target_grads: bfloat16 [128, 16384], P('ex', 'feat'), may hold values from -300 to 300
- target_mass: float32 [128], replicated, may hold values from 0.25 to 4
Outputs:
- mixtures: bfloat16 [128, 16384], P('ex', 'feat')
All inputs are finite; a program needn't handle non-finite values.
Results may differ from a plain program's by a relative error of at most 0.0048.
Values may be sent and summed in bfloat16 or wider, within the bound.
A program may use at most 64 MiB of HBM per device.

v0:
```python
import math

import jax
import jax.numpy as jnp
from jax import lax
from jax.sharding import PartitionSpec as P

F = 16384
ITERS = 3


def merged(part, axis, combine):
    gathered = jax.tree.map(lambda a: lax.all_gather(a, axis), part)

    def take(source):
        return jax.tree.map(lambda a: lax.dynamic_index_in_dim(a, source, 0, False), gathered)

    return lax.fori_loop(
        1, lax.axis_size(axis), lambda source, state: combine(state, take(source)), take(0)
    )


def pair_combine(first, second):
    top = jnp.maximum(first[0], second[0])
    total = first[1] * jnp.exp(first[0] - top) + second[1] * jnp.exp(second[0] - top)
    return (top, total)


def column_lse(values):
    local_max = jnp.max(values, axis=0)
    local_sum = jnp.sum(jnp.exp(values - local_max[None, :]), axis=0)
    top, total = merged((local_max, local_sum), "ex", pair_combine)
    return top + jnp.log(total)


def row_lse_local(values):
    top = jnp.max(values, axis=1)
    return top + jnp.log(jnp.sum(jnp.exp(values - top[:, None]), axis=1))


def shards(train_grads, target_grads, target_mass):
    rows = train_grads.shape[0]
    my_targets = target_grads.shape[0]
    total_rows = rows * lax.axis_size("ex")
    scale = 3.0 / math.sqrt(F)
    log_a = -math.log(total_rows)
    partial_value = lax.dot_general(
        train_grads,
        lax.all_gather(target_grads, "ex", axis=0, tiled=True),
        (((1,), (1,)), ((), ())),
        preferred_element_type=jnp.float32,
    )
    mass_total = jnp.sum(target_mass)
    weights = target_mass / mass_total
    log_b = jnp.log(target_mass) - jnp.log(mass_total)
    logits = lax.psum(partial_value, "feat") * scale
    col_pot = jnp.zeros(log_b.shape, jnp.float32)
    row_pot = jnp.zeros((rows,), jnp.float32)
    for step in range(ITERS):
        row_pot = log_a - row_lse_local(logits + col_pot[None, :])
        col_pot = log_b - column_lse(logits + row_pot[:, None])
    plan = jnp.exp(logits + row_pot[:, None] + col_pot[None, :]).astype(jnp.bfloat16)
    mixed = lax.psum_scatter(
        lax.dot_general(
            plan, train_grads, (((0,), (0,)), ((), ())), preferred_element_type=jnp.float32
        ),
        "ex",
        scatter_dimension=0,
        tiled=True,
    )
    my_start = lax.axis_index("ex") * my_targets
    my_weights = lax.dynamic_slice_in_dim(weights, my_start, my_targets)
    return (mixed / my_weights[:, None]).astype(jnp.bfloat16)


def solution(mesh):
    return jax.shard_map(
        shards,
        mesh=mesh,
        in_specs=(P("ex", "feat"), P("ex", "feat"), P()),
        out_specs=P("ex", "feat"),
        check_vma=False,
    )
```

profile of v0, /device:TPU:0, one launch (start us, length us, event | category | flops | bytes accessed | tf_op | source)
XLA Modules:
  0.0 203.3 jit_solution(10879833688206655125)
XLA Ops:
  6.5 0.7 all-gather.14.cloned.1.call-update
  7.3 28.2 %all-gather.14.cloned.1.call-done = bf16[128,4096]{1,0:T(8,128)(2,1)} async-done(((bf16[16,4096]{1,0:T(8,128)(2,1)}), bf16[128,4096]{1,0:T(8,128)(2,1)}) %all-gather.14.cloned.1.call-update) | async-done | bytes 1048592 | tf_op jit(solution)/shard_map/all_gather | solution.py:49
  35.5 6.8 %fusion.11 = f32[1024,128]{1,0:T(8,128)} fusion(bf16[1024,4096]{1,0:T(8,128)(2,1)} %param.9, bf16[128,4096]{1,0:T(8,128)(2,1)} %all-gather.14.cloned.1.call-done), kind=kOutput, calls=%fused_computation.51 | convolution fusion | flops 1073741824 | bytes 9961472 | tf_op jit(solution)/shard_map/dot_general | solution.py:47
  42.3 0.0 reduce-scatter.2.cloned.1.call-start
  42.3 0.6 reduce_sum.63
  43.6 37.1 %all-reduce.2.cloned.1.call-done = f32[1024,128]{1,0:T(8,128)} async-done(((f32[1024,128]{1,0:T(8,128)}), f32[1024,128]{1,0:T(8,128)}) %all-reduce.2.cloned.1.call-update) | async-done | bytes 524304 | tf_op jit(solution)/shard_map/psum | solution.py:56
  80.7 1.2 fusion.9
  82.0 1.4 exponential_reduce_fusion.5
  83.4 1.3 add_reduce_fusion.3
  84.7 8.7 %all-gather.6 = f32[8,1,128]{2,1,0:T(1,128)S(1)} all-gather(f32[1,1,128]{2,1,0:T(1,128)S(1)} %bitcast.76), channel_id=2, replica_groups=mesh['ex'=8,'feat'=4] {'ex'}, dimensions={0}, use_global_device_ids=true | all-gather | bytes 4608 | tf_op jit(solution)/shard_map/all_gather | solution.py:13
  93.4 1.3 exponential_reduce_fusion.4
  94.6 8.7 %all-gather.7 = f32[8,1,128]{2,1,0:T(1,128)S(1)} all-gather(f32[1,1,128]{2,1,0:T(1,128)S(1)} %bitcast.78), channel_id=3, replica_groups=mesh['ex'=8,'feat'=4] {'ex'}, dimensions={0}, use_global_device_ids=true | all-gather | bytes 4608 | tf_op jit(solution)/shard_map/all_gather | solution.py:13
  103.3 0.3 while.51
  103.6 1.3 add_reduce_fusion.2
  104.9 1.4 exponential_reduce_fusion.3
  106.3 1.3 add_reduce_fusion.1
  107.6 7.8 %all-gather.8 = f32[8,1,128]{2,1,0:T(1,128)S(1)} all-gather(f32[1,1,128]{2,1,0:T(1,128)S(1)} %bitcast.77), channel_id=4, replica_groups=mesh['ex'=8,'feat'=4] {'ex'}, dimensions={0}, use_global_device_ids=true | all-gather | bytes 4608 | tf_op jit(solution)/shard_map/all_gather | solution.py:13
  115.4 1.3 exponential_reduce_fusion.2
  116.6 8.7 %all-gather.9 = f32[8,1,128]{2,1,0:T(1,128)S(1)} all-gather(f32[1,1,128]{2,1,0:T(1,128)S(1)} %bitcast.79), channel_id=5, replica_groups=mesh['ex'=8,'feat'=4] {'ex'}, dimensions={0}, use_global_device_ids=true | all-gather | bytes 4608 | tf_op jit(solution)/shard_map/all_gather | solution.py:13
  125.3 0.3 while.52
  125.6 0.6 broadcast_divide_fusion
  126.3 1.3 add_reduce_fusion
  127.5 1.4 exponential_reduce_fusion.1
  128.9 1.3 add_reduce_fusion.4
  130.2 1.3 exponential_reduce_fusion
  131.5 7.8 %all-gather.11 = f32[8,1,128]{2,1,0:T(1,128)S(1)} all-gather(f32[1,1,128]{2,1,0:T(1,128)S(1)} %bitcast.80), channel_id=7, replica_groups=mesh['ex'=8,'feat'=4] {'ex'}, dimensions={0}, use_global_device_ids=true | all-gather | bytes 4608 | tf_op jit(solution)/shard_map/all_gather | solution.py:13
  139.3 8.7 %all-gather.10 = f32[8,1,128]{2,1,0:T(1,128)S(1)} all-gather(f32[1,1,128]{2,1,0:T(1,128)S(1)} %bitcast.75), channel_id=6, replica_groups=mesh['ex'=8,'feat'=4] {'ex'}, dimensions={0}, use_global_device_ids=true | all-gather | bytes 4608 | tf_op jit(solution)/shard_map/all_gather | solution.py:13
  147.9 0.3 while.53
  148.3 6.3 %fusion.6 = f32[128,4096]{1,0:T(8,128)} fusion(bf16[1024,4096]{1,0:T(8,128)(2,1)} %param.9, f32[128]{0:T(128)S(1)} %add_subtract_fusion.3, f32[1024]{0:T(1024)S(1)} %add_subtract_fusion, f32[1024,128]{1,0:T(8,128)} %all-reduce.2.cloned.1.call-done), kind=kOutput, calls=%fused_computation.30 | convolution fusion | flops 1074266112 | bytes 11014656 | tf_op jit(solution)/shard_map/dot_general | solution.py:64
  154.6 0.1 dynamic_slice.88
  154.7 40.4 %reduce-scatter.2.cloned.1.call-done = f32[16,4096]{1,0:T(8,128)} async-done(((f32[128,4096]{1,0:T(8,128)}), f32[16,4096]{1,0:T(8,128)}) %reduce-scatter.2.cloned.1.call-update) | async-done | bytes 262160 | tf_op jit(solution)/shard_map/reduce_scatter | solution.py:63
  195.0 1.7 divide_convert_fusion
  (38 shorter events, 0.7 us)
Async XLA Ops:
  6.5 35.8 %copy-start = (f32[128]{0:T(128)S(1)}, f32[128]{0:T(128)}, u32[]{:S(2)}) copy-start(f32[128]{0:T(128)} %param.11) | copy-start | bytes 1540
  6.5 28.9 %all-gather.14.cloned.1.call-start = ((), (), s32[]{:S(2)}) async-start(), calls=%async_computation.1 | async-start | bytes 1179648 | tf_op jit(solution)/shard_map/all_gather | solution.py:49
  7.3 73.5 %all-reduce.2.cloned.1.call-start = ((), (), s32[]{:S(2)}) async-start(), calls=%async_computation.2 | async-start | bytes 1048576 | tf_op jit(solution)/shard_map/psum | solution.py:56
  42.3 152.8 %reduce-scatter.2.cloned.1.call-start = ((), (), s32[]{:S(2)}) async-start(), calls=%async_computation.3 | async-start | bytes 2359296 | tf_op jit(solution)/shard_map/reduce_scatter | solution.py:63
Sparse Core Ops, SparseCore 0:
  9.2 26.1 all-gather.13
  42.4 38.2 all-reduce.1
  154.7 40.2 reduce-scatter.1
where the time goes:
time: 204 us; the launch traced here: 203 us
  waiting for transfers between devices  106 us (52%)
  blocking collectives  50.4 us (25%)
  other arithmetic  19.1 us (9%)
  between operations  13.9 us (7%)
  matrix products  13.1 us (6%)
    all_gather x6, blocking collectives, merged(): gathered = jax.tree.map(lambda a: lax.all_gather(a, axis), part)  50.4 us
    reduce_scatter x1, waiting for transfers between devices, shards(): lax.psum_scatter(lax.dot_general(plan, train_grads, (((0,), (0,)), ((), (...  40.4 us
    psum x1, waiting for transfers between devices, shards(): logits = lax.psum(partial_value, 'feat') * scale  37.1 us
    all_gather x1, waiting for transfers between devices, shards(): lax.all_gather(target_grads, 'ex', axis=0, tiled=True)  28.2 us
    dot_general x1, matrix products, shards(): lax.dot_general(train_grads, lax.all_gather(target_grads, 'ex', axis=0, t...  6.76 us
    dot_general x1, matrix products, shards(): lax.dot_general(plan, train_grads, (((0,), (0,)), ((), ())), preferred_el...  6.3 us
    reduce_sum x3, other arithmetic, row_lse_local(): return top + jnp.log(jnp.sum(jnp.exp(values - top[:, None]), axis=1))  4.21 us
  transfers between devices with their start and end apart: 3, of which 3 were waited for; matrix products, arithmetic and copies ran while one was open for 0% of the time, Pallas kernels for 0%

commit v1 on v0

v1 whole, which is shorter than its diff:
```python
import functools
import math

import jax
import jax.numpy as jnp
from jax import lax
from jax.experimental import pallas as pl
from jax.experimental.pallas import tpu as pltpu
from jax.sharding import PartitionSpec as P

ITERS = 3
MESH = pl.DeviceIdType.MESH


def remote(src, dst, send, recv, axis, peer):
    return pltpu.make_async_remote_copy(
        src_ref=src,
        dst_ref=dst,
        send_sem=send,
        recv_sem=recv,
        device_id={axis: peer},
        device_id_type=MESH,
    )


def kernel(
    n, nf, chunks,
    train_hbm, target, mass_row, mass_col, out,
    train, tg, part, rs, logits, plan_t, macc, mb, mr, st_send, st_recv,
    load_sem, g_send, g_recv, r_send, r_recv, a_send, a_recv, s_send, s_recv, m_send, m_recv,
):
    me = lax.axis_index("ex")
    mf = lax.axis_index("feat")
    rows, depth = train.shape
    nt = tg.shape[0]
    t = target.shape[0]
    dc = depth // chunks
    rf = rows // nf
    scale = 3.0 / math.sqrt(depth * nf)
    log_a = -math.log(rows * n)

    def ex_at(k):
        return lax.rem(me + k, n)

    def feat_at(k):
        return lax.rem(mf + k, nf)

    def block(index, size):
        return pl.ds(pl.multiple_of(index * size, size), size)

    loads = []
    for c in range(chunks):
        cols = pl.ds(c * dc, dc)
        loads.append(
            pltpu.make_async_copy(train_hbm.at[:, cols], train.at[:, cols], load_sem.at[c])
        )
        loads[-1].start()

    barrier = pltpu.get_barrier_semaphore()
    for k in range(1, n):
        pl.semaphore_signal(barrier, inc=1, device_id={"ex": ex_at(k)}, device_id_type=MESH)
    for k in range(1, nf):
        pl.semaphore_signal(barrier, inc=1, device_id={"feat": feat_at(k)}, device_id_type=MESH)
    pl.semaphore_wait(barrier, n + nf - 2)

    gathers = []
    for c in range(chunks):
        cols = pl.ds(c * dc, dc)
        for k in range(1, n):
            copy = remote(
                target.at[:, cols], tg.at[block(me, t), cols],
                g_send.at[c, k], g_recv.at[c, k], "ex", ex_at(k),
            )
            copy.start()
            gathers.append(copy)
    tg[block(me, t), :] = target[...]

    mass_total = jnp.sum(mass_row[...], axis=1, keepdims=True)
    log_b = jnp.log(mass_row[...]) - jnp.log(mass_total)

    def score(c, index):
        where = block(index, rf)
        value = lax.dot_general(
            train[where, c * dc:(c + 1) * dc],
            tg[:, c * dc:(c + 1) * dc],
            (((1,), (1,)), ((), ())),
            preferred_element_type=jnp.float32,
        )
        if c == 0:
            part[where, :] = value
        else:
            part[where, :] += value

    reduces = []
    for c in range(chunks):
        loads[c].wait()
        for k in range(1, n):
            gathers[c * (n - 1) + k - 1].wait_recv()
        if c < chunks - 1:
            @pl.loop(0, nf)
            def _(index):
                score(c, index)
        else:
            for k in range(1, nf):
                score(c, feat_at(k))
                copy = remote(
                    part.at[block(feat_at(k), rf)], rs.at[k], r_send.at[k], r_recv.at[k], "feat", feat_at(k)
                )
                copy.start()
                reduces.append(copy)
            score(c, mf)
    for copy in reduces:
        copy.wait_recv()
    own = part[block(mf, rf), :]
    for k in range(1, nf):
        own = own + rs[k]
    logits[block(mf, rf), :] = own * scale
    spreads = []
    for k in range(1, nf):
        copy = remote(
            logits.at[block(mf, rf)], logits.at[block(mf, rf)], a_send.at[k], a_recv.at[k], "feat", feat_at(k)
        )
        copy.start()
        spreads.append(copy)
    for copy in spreads:
        copy.wait_recv()

    col_pot = jnp.zeros((1, nt), jnp.float32)
    stats = []
    row_pot = None
    for step in range(ITERS):
        value = logits[...] + col_pot
        top = jnp.max(value, axis=1, keepdims=True)
        row_pot = log_a - (top + jnp.log(jnp.sum(jnp.exp(value - top), axis=1, keepdims=True)))
        value = logits[...] + row_pot
        top = jnp.max(value, axis=0, keepdims=True)
        total = jnp.sum(jnp.exp(value - top), axis=0, keepdims=True)
        st_send[step, 0:1, :] = top
        st_send[step, 1:2, :] = total
        wave = []
        for k in range(1, n):
            copy = remote(
                st_send.at[step], st_recv.at[step, me],
                s_send.at[step, k], s_recv.at[step, k], "ex", ex_at(k),
            )
            copy.start()
            wave.append(copy)
        st_recv[step, me] = st_send[step]
        for copy in wave:
            copy.wait_recv()
        stats += wave
        tops = st_recv[step, :, 0, :]
        totals = st_recv[step, :, 1, :]
        top = jnp.max(tops, axis=0, keepdims=True)
        total = jnp.sum(totals * jnp.exp(tops - top), axis=0, keepdims=True)
        col_pot = log_b - (top + jnp.log(total))

    plan = jnp.exp(logits[...] + row_pot + col_pot)
    plan_t[...] = plan.T.astype(jnp.bfloat16)

    tile = math.gcd(dc, 256)
    mixes = []
    for c in range(chunks):
        cols = pl.ds(c * dc, dc)

        @pl.loop(0, dc // tile)
        def _(index):
            where = pl.ds(pl.multiple_of(c * dc + index * tile, tile), tile)
            value = jnp.dot(plan_t[...], train[:, where], preferred_element_type=jnp.float32)
            macc[:, where] = value
            mb[:, where] = value.astype(jnp.bfloat16)

        for k in range(1, n):
            copy = remote(
                mb.at[block(ex_at(k), t), cols], mr.at[me, :, cols],
                m_send.at[c, k], m_recv.at[c, k], "ex", ex_at(k),
            )
            copy.start()
            mixes.append(copy)

    weight = mass_col[block(me, t), :] / mass_total
    for c in range(chunks):
        for k in range(1, n):
            mixes[c * (n - 1) + k - 1].wait_recv()
        total = macc[block(me, t), c * dc:(c + 1) * dc]
        for k in range(1, n):
            total = total + mr[ex_at(k), :, c * dc:(c + 1) * dc].astype(jnp.float32)
        out[:, c * dc:(c + 1) * dc] = (total / weight).astype(jnp.bfloat16)
    for copy in gathers + reduces + spreads + stats + mixes:
        copy.wait_send()


def shards(train_grads, target_grads, target_mass):
    n, nf = lax.axis_size("ex"), lax.axis_size("feat")
    rows, depth = train_grads.shape
    t = target_grads.shape[0]
    nt = t * n
    chunks = 4 if depth % 512 == 0 else 1
    f32, bf16 = jnp.float32, jnp.bfloat16
    vmem = pl.BlockSpec(memory_space=pltpu.VMEM)
    dma = pltpu.SemaphoreType.DMA
    return pl.pallas_call(
        functools.partial(kernel, n, nf, chunks),
        out_shape=jax.ShapeDtypeStruct((t, depth), bf16),
        in_specs=[pl.BlockSpec(memory_space=pl.ANY), vmem, vmem, vmem],
        out_specs=vmem,
        scratch_shapes=[
            pltpu.VMEM((rows, depth), bf16),
            pltpu.VMEM((nt, depth), bf16),
            pltpu.VMEM((rows, nt), f32),
            pltpu.VMEM((nf, rows // nf, nt), f32),
            pltpu.VMEM((rows, nt), f32),
            pltpu.VMEM((nt, rows), bf16),
            pltpu.VMEM((nt, depth), f32),
            pltpu.VMEM((nt, depth), bf16),
            pltpu.VMEM((n, t, depth), bf16),
            pltpu.VMEM((ITERS, 8, nt), f32),
            pltpu.VMEM((ITERS, n, 8, nt), f32),
            dma((chunks,)),
            dma((chunks, n)), dma((chunks, n)),
            dma((nf,)), dma((nf,)),
            dma((nf,)), dma((nf,)),
            dma((ITERS, n)), dma((ITERS, n)),
            dma((chunks, n)), dma((chunks, n)),
        ],
        compiler_params=pltpu.CompilerParams(
            collective_id=0, has_side_effects=True, vmem_limit_bytes=48 * 1024 * 1024
        ),
        cost_estimate=pl.CostEstimate(
            flops=4 * rows * nt * depth,
            bytes_accessed=2 * rows * depth,
            transcendentals=7 * rows * nt,
        ),
    )(train_grads, target_grads, target_mass.reshape(1, nt), target_mass.reshape(nt, 1))


def solution(mesh):
    return jax.shard_map(
        shards,
        mesh=mesh,
        in_specs=(P("ex", "feat"), P("ex", "feat"), P()),
        out_specs=P("ex", "feat"),
        check_vma=False,
    )
```

time: 204 us -> 72.5 us (0.36)
  waiting for transfers between devices: 106 us -> 0 us
  Pallas kernels: 0 us -> 68.1 us
  blocking collectives: 50.4 us -> 0 us
  other arithmetic: 19.1 us -> 0 us
  between operations: 13.9 us -> 0.02 us
  matrix products: 13.1 us -> 0 us
  local copies, waits for them, and re-layouts: 0.09 us -> 2.97 us
    pallas_call x0 -> x1, Pallas kernels: none -> 68.1 us  [shards(): pl.pallas_call(functools.partial(kernel, n, nf, chunks), out_shape=jax.Sh...]
    all_gather x6 -> x0, blocking collectives: 50.4 us -> none  [merged(): gathered = jax.tree.map(lambda a: lax.all_gather(a, axis), part)]
    reduce_scatter x1 -> x0, waiting for transfers between devices: 40.4 us -> none  [shards(): lax.psum_scatter(lax.dot_general(plan, train_grads, (((0,), (0,)), ((), (...]
    psum x1 -> x0, waiting for transfers between devices: 37.1 us -> none  [shards(): logits = lax.psum(partial_value, 'feat') * scale]
    all_gather x1 -> x0, waiting for transfers between devices: 28.2 us -> none  [shards(): lax.all_gather(target_grads, 'ex', axis=0, tiled=True)]
    dot_general x2 -> x0, matrix products: 13.1 us -> none  [the longest x1 6.76 us: shards(): lax.dot_general(train_grads, lax.all_gather(target_grads, 'ex', axis=0, t...]
    reduce_sum x7 -> x0, other arithmetic: 8.63 us -> none  [the longest x3 4.21 us: row_lse_local(): return top + jnp.log(jnp.sum(jnp.exp(values - top[:, None]), axis=1))]
    reduce_max x6 -> x0, other arithmetic: 7.52 us -> none  [the longest x3 3.77 us: column_lse(): local_max = jnp.max(values, axis=0)]
  transfers between devices with their start and end apart: 3 -> 0, of which waited for: 3 -> 0; matrix products, arithmetic and copies ran while one was open for 0% -> 0% of each run, Pallas kernels for 0% -> 0%
where the time goes in v1:
time: 72.5 us; the launch traced here: 71.1 us
  Pallas kernels  68.1 us (94%)
  local copies, waits for them, and re-layouts  2.97 us (4%)
    pallas_call x1, Pallas kernels, shards(): pl.pallas_call(functools.partial(kernel, n, nf, chunks), out_shape=jax.Sh...  68.1 us
    unnamed x5, local copies, waits for them, and re-layouts  2.21 us

profile of v1, /device:TPU:0, one launch (start us, length us, event | category | flops | bytes accessed | tf_op | source)
XLA Modules:
  0.0 71.1 jit_solution(3742857078608803654)
XLA Ops:
  0.0 0.8 %copy.4.mass_col = f32[128,1]{1,0:T(8,128)S(1)} copy(f32[128,1]{0,1:T(1,128)} %bitcast.2) | data formatting | bytes 1024 | tf_op jit(solution)/shard_map/reshape | solution.py:234
  0.8 0.0 copy-start
  0.8 0.9 %copy-done = bf16[16,4096]{1,0:T(8,128)(2,1)S(1)} copy-done((bf16[16,4096]{1,0:T(8,128)(2,1)S(1)}, bf16[16,4096]{1,0:T(8,128)(2,1)}, u32[]{:S(2)}) %copy-start) | copy-done | bytes 131096
  1.7 0.0 copy-start.1
  1.7 0.7 copy-done.1
  2.3 68.1 %shard_map.37 = bf16[16,4096]{1,0:T(8,128)(2,1)S(1)} custom-call(bf16[1024,4096]{1,0:T(8,128)(2,1)} %train_hbm.1, bf16[16,4096]{1,0:T(8,128)(2,1)S(1)} %copy-done, f32[1,128]{1,0:T(1,128)S(1)} %bitcast.3, f32[128,1]{1,0:T(8,128)S(1)} %copy.4.mass_col), custom_call_target="tpu_custom_call" | custom-call | flops 2147483648 | bytes 8388608 | tf_op jit(solution)/shard_map/pallas_call | solution.py:202
  70.4 0.7 copy.6
Async XLA Ops:
  0.8 0.9 %copy-start = (bf16[16,4096]{1,0:T(8,128)(2,1)S(1)}, bf16[16,4096]{1,0:T(8,128)(2,1)}, u32[]{:S(2)}) copy-start(bf16[16,4096]{1,0:T(8,128)(2,1)} %target.1) | copy-start | bytes 393220
  1.7 0.7 copy-start.1

commit v2 on v1

v2 whole, which is shorter than its diff:
```python
import functools
import math

import jax
import jax.numpy as jnp
from jax import lax
from jax.experimental import pallas as pl
from jax.experimental.pallas import tpu as pltpu
from jax.sharding import PartitionSpec as P

ITERS = 3
MESH = pl.DeviceIdType.MESH


def remote(src, dst, send, recv, axis, peer):
    return pltpu.make_async_remote_copy(
        src_ref=src,
        dst_ref=dst,
        send_sem=send,
        recv_sem=recv,
        device_id={axis: peer},
        device_id_type=MESH,
    )


def kernel(
    n, nf, chunks,
    train_hbm, target, mass_hbm, out,
    train, tg, part, rs, plan_t, macc, mb, xr, cb, mr, mass_row, mass_col,
    ft_send, ft_recv, ex_send, ex_recv,
    load_sem, own_sem, mass_sem, g_send, g_recv, f_send, f_recv, r_send, r_recv,
    t_send, t_recv, s_send, s_recv, a_send, a_recv, x_send, x_recv, m_send, m_recv,
):
    me = lax.axis_index("ex")
    mf = lax.axis_index("feat")
    rows, depth = train.shape
    nt = tg.shape[0]
    t = target.shape[0]
    dc = depth // chunks
    rf = rows // nf
    nq = n // 2
    q = me // 2
    core = lax.rem(me, 2)
    sibling = me + 1 - 2 * core
    scale = 3.0 / math.sqrt(depth * nf)
    log_a = -math.log(rows * n)

    def ex_at(k):
        return lax.rem(me + k, n)

    def feat_at(k):
        return lax.rem(mf + k, nf)

    def chip_at(j):
        return lax.rem(q + j, nq)

    def chip_from(j):
        return lax.rem(q - j + nq, nq)

    def block(index, size):
        return pl.ds(pl.multiple_of(index * size, size), size)

    def span(c):
        return pl.ds(c * dc, dc)

    mass_load = pltpu.make_async_copy(mass_hbm, mass_row, mass_sem)
    mass_load.start()
    own_load = pltpu.make_async_copy(target, tg.at[block(me, t)], own_sem)
    own_load.start()
    loads = []
    for c in range(chunks):
        loads.append(
            pltpu.make_async_copy(train_hbm.at[:, span(c)], train.at[:, span(c)], load_sem.at[c])
        )
        loads[-1].start()

    barrier = pltpu.get_barrier_semaphore()
    for k in range(1, n):
        pl.semaphore_signal(barrier, inc=1, device_id={"ex": ex_at(k)}, device_id_type=MESH)
    for k in range(1, nf):
        pl.semaphore_signal(barrier, inc=1, device_id={"feat": feat_at(k)}, device_id_type=MESH)
    pl.semaphore_wait(barrier, n + nf - 2)

    gathers = []
    forwards = []
    for c in range(chunks):
        for j in range(1, nq):
            copy = remote(
                target.at[:, span(c)], tg.at[block(me, t), span(c)],
                g_send.at[c, j], g_recv.at[c, j], "ex", 2 * chip_at(j) + core,
            )
            copy.start()
            gathers.append(copy)
        copy = remote(
            target.at[:, span(c)], tg.at[block(me, t), span(c)],
            f_send.at[c, 0], f_recv.at[c, 0], "ex", sibling,
        )
        copy.start()
        forwards.append([copy])

    mass_load.wait()
    mass_total = jnp.sum(mass_row[...], axis=1, keepdims=True)
    log_b = jnp.log(mass_row[...]) - jnp.log(mass_total)
    mass_col[...] = jnp.broadcast_to(mass_row[...] / mass_total, (8, nt)).T
    own_load.wait()

    def forward(c):
        for j in range(1, nq):
            gathers[c * (nq - 1) + j - 1].wait_recv()
            where = block(2 * chip_from(j) + core, t)
            copy = remote(
                tg.at[where, span(c)], tg.at[where, span(c)],
                f_send.at[c, j], f_recv.at[c, j], "ex", sibling,
            )
            copy.start()
            forwards[c].append(copy)

    def score(c, index):
        where = block(index, rf)
        value = lax.dot_general(
            train[where, c * dc:(c + 1) * dc],
            tg[:, c * dc:(c + 1) * dc],
            (((1,), (1,)), ((), ())),
            preferred_element_type=jnp.float32,
        )
        if c == 0:
            part[where, :] = value
        else:
            part[where, :] += value

    reduces = []
    forward(0)
    for c in range(chunks):
        if c + 1 < chunks:
            forward(c + 1)
        loads[c].wait()
        for copy in forwards[c]:
            copy.wait_recv()
        if c < chunks - 1:
            @pl.loop(0, nf)
            def _(index):
                score(c, index)
        else:
            for k in range(1, nf):
                score(c, feat_at(k))
                copy = remote(
                    part.at[block(feat_at(k), rf)], rs.at[k],
                    r_send.at[k], r_recv.at[k], "feat", feat_at(k),
                )
                copy.start()
                reduces.append(copy)
            score(c, mf)
    logits = part[block(mf, rf), :]
    for copy in reduces:
        copy.wait_recv()
    for k in range(1, nf):
        logits = logits + rs[k]
    logits = logits * scale
    part[block(mf, rf), :] = logits

    def exchange(step, axis, send, recv, here, at, size, send_sem, recv_sem, top, total):
        send[step, 0:1, :] = top
        send[step, 1:2, :] = total
        wave = []
        for k in range(1, size):
            copy = remote(
                send.at[step], recv.at[step, here],
                send_sem.at[step, k], recv_sem.at[step, k], axis, at(k),
            )
            copy.start()
            wave.append(copy)
        recv[step, here] = send[step]
        for copy in wave:
            copy.wait_recv()
        tops = recv[step, :, 0, :]
        top = jnp.max(tops, axis=0, keepdims=True)
        total = jnp.sum(recv[step, :, 1, :] * jnp.exp(tops - top), axis=0, keepdims=True)
        return top, total, wave

    col_pot = jnp.zeros((1, nt), jnp.float32)
    stats = []
    row_pot = None
    for step in range(ITERS):
        value = logits + col_pot
        top = jnp.max(value, axis=1, keepdims=True)
        row_pot = log_a - (top + jnp.log(jnp.sum(jnp.exp(value - top), axis=1, keepdims=True)))
        value = logits + row_pot
        top = jnp.max(value, axis=0, keepdims=True)
        total = jnp.sum(jnp.exp(value - top), axis=0, keepdims=True)
        top, total, wave = exchange(
            step, "feat", ft_send, ft_recv, mf, feat_at, nf, t_send, t_recv, top, total
        )
        stats += wave
        top, total, wave = exchange(
            step, "ex", ex_send, ex_recv, me, ex_at, n, s_send, s_recv, top, total
        )
        stats += wave
        col_pot = log_b - (top + jnp.log(total))

    plan_t[mf] = jnp.exp(logits + row_pot + col_pot).T.astype(jnp.bfloat16)
    spreads = []
    for k in range(1, nf):
        copy = remote(
            plan_t.at[mf], plan_t.at[mf], a_send.at[k], a_recv.at[k], "feat", feat_at(k)
        )
        copy.start()
        spreads.append(copy)
    for copy in spreads:
        copy.wait_recv()

    tile = math.gcd(dc, 256)
    swaps = []
    mixes = []

    def mix(c):
        @pl.loop(0, dc // tile)
        def _(index):
            where = pl.ds(pl.multiple_of(c * dc + index * tile, tile), tile)
            value = jnp.zeros((nt, tile), jnp.float32)
            for f in range(nf):
                value += jnp.dot(
                    plan_t[f], train[f * rf:(f + 1) * rf, where],
                    preferred_element_type=jnp.float32,
                )
            value = value.reshape(nq, 2, t, tile)
            macc[:, :, :, where] = value
            mb[:, :, :, where] = value.astype(jnp.bfloat16)

        copy = remote(
            mb.at[:, 1 - core, :, span(c)], xr.at[:, :, span(c)],
            x_send.at[c], x_recv.at[c], "ex", sibling,
        )
        copy.start()
        swaps.append(copy)

    def send_on(c):
        cols = slice(c * dc, (c + 1) * dc)
        swaps[c].wait_recv()
        total = macc[:, core, :, cols] + xr[:, :, cols].astype(jnp.float32)
        cb[:, :, cols] = total.astype(jnp.bfloat16)
        for j in range(1, nq):
            copy = remote(
                cb.at[chip_at(j), :, span(c)], mr.at[q, :, span(c)],
                m_send.at[c, j], m_recv.at[c, j], "ex", 2 * chip_at(j) + core,
            )
            copy.start()
            mixes.append(copy)

    for c in range(chunks):
        mix(c)
        if c > 0:
            send_on(c - 1)
    send_on(chunks - 1)

    weight = mass_col[block(me, t), 0:1]
    for c in range(chunks):
        cols = slice(c * dc, (c + 1) * dc)
        total = macc[q, core, :, cols] + xr[q, :, cols].astype(jnp.float32)
        for j in range(1, nq):
            mixes[c * (nq - 1) + j - 1].wait_recv()
        for j in range(1, nq):
            total = total + mr[chip_at(j), :, cols].astype(jnp.float32)
        out[:, cols] = (total / weight).astype(jnp.bfloat16)
    for group in forwards:
        for copy in group:
            copy.wait_send()
    for copy in gathers + reduces + spreads + stats + swaps + mixes:
        copy.wait_send()


def shards(train_grads, target_grads, target_mass):
    n, nf = lax.axis_size("ex"), lax.axis_size("feat")
    rows, depth = train_grads.shape
    t = target_grads.shape[0]
    nt = t * n
    nq = n // 2
    chunks = 4 if depth % 512 == 0 else 1
    f32, bf16 = jnp.float32, jnp.bfloat16
    vmem = pl.BlockSpec(memory_space=pltpu.VMEM)
    anywhere = pl.BlockSpec(memory_space=pl.ANY)
    dma = pltpu.SemaphoreType.DMA
    return pl.pallas_call(
        functools.partial(kernel, n, nf, chunks),
        out_shape=jax.ShapeDtypeStruct((t, depth), bf16),
        in_specs=[anywhere, anywhere, anywhere],
        out_specs=vmem,
        scratch_shapes=[
            pltpu.VMEM((rows, depth), bf16),
            pltpu.VMEM((nt, depth), bf16),
            pltpu.VMEM((rows, nt), f32),
            pltpu.VMEM((nf, rows // nf, nt), f32),
            pltpu.VMEM((nf, nt, rows // nf), bf16),
            pltpu.VMEM((nq, 2, t, depth), f32),
            pltpu.VMEM((nq, 2, t, depth), bf16),
            pltpu.VMEM((nq, t, depth), bf16),
            pltpu.VMEM((nq, t, depth), bf16),
            pltpu.VMEM((nq, t, depth), bf16),
            pltpu.VMEM((1, nt), f32),
            pltpu.VMEM((nt, 8), f32),
            pltpu.VMEM((ITERS, 8, nt), f32),
            pltpu.VMEM((ITERS, nf, 8, nt), f32),
            pltpu.VMEM((ITERS, 8, nt), f32),
            pltpu.VMEM((ITERS, n, 8, nt), f32),
            dma((chunks,)), dma, dma,
            dma((chunks, nq)), dma((chunks, nq)),
            dma((chunks, nq)), dma((chunks, nq)),
            dma((nf,)), dma((nf,)),
            dma((ITERS, nf)), dma((ITERS, nf)),
            dma((ITERS, n)), dma((ITERS, n)),
            dma((nf,)), dma((nf,)),
            dma((chunks,)), dma((chunks,)),
            dma((chunks, nq)), dma((chunks, nq)),
        ],
        compiler_params=pltpu.CompilerParams(
            collective_id=0, has_side_effects=True, vmem_limit_bytes=48 * 1024 * 1024
        ),
        cost_estimate=pl.CostEstimate(
            flops=4 * rows * nt * depth,
            bytes_accessed=2 * rows * depth,
            transcendentals=7 * rows * nt,
        ),
    )(train_grads, target_grads, target_mass.reshape(1, nt))


def solution(mesh):
    return jax.shard_map(
        shards,
        mesh=mesh,
        in_specs=(P("ex", "feat"), P("ex", "feat"), P()),
        out_specs=P("ex", "feat"),
        check_vma=False,
    )
```

time: 72.5 us -> 70.2 us (0.968); the launches traced: 71.1 us -> 70.1 us
  local copies, waits for them, and re-layouts: 2.97 us -> 2.22 us
    reshape x1 -> x0, local copies, waits for them, and re-layouts: 0.76 us -> none  [shards(): target_mass.reshape(nt, 1)]
where the time goes in v2:
time: 70.2 us; the launch traced here: 70.1 us
  Pallas kernels  67.8 us (97%)
  local copies, waits for them, and re-layouts  2.22 us (3%)
    pallas_call x1, Pallas kernels, shards(): pl.pallas_call(functools.partial(kernel, n, nf, chunks), out_shape=jax.Sh...  67.8 us
    unnamed x5, local copies, waits for them, and re-layouts  2.22 us

profile of v2, /device:TPU:0, one launch (start us, length us, event | category | flops | bytes accessed | tf_op | source)
XLA Modules:
  0.0 70.1 jit_solution(13923132297651491393)
XLA Ops:
  0.0 0.0 copy-start
  0.0 0.9 %copy-done = bf16[16,4096]{1,0:T(8,128)(2,1)S(1)} copy-done((bf16[16,4096]{1,0:T(8,128)(2,1)S(1)}, bf16[16,4096]{1,0:T(8,128)(2,1)}, u32[]{:S(2)}) %copy-start) | copy-done | bytes 131096
  0.9 0.0 copy-start.1
  0.9 0.7 copy-done.1
  1.6 67.8 %shard_map.37 = bf16[16,4096]{1,0:T(8,128)(2,1)S(1)} custom-call(bf16[1024,4096]{1,0:T(8,128)(2,1)} %train_hbm.1, bf16[16,4096]{1,0:T(8,128)(2,1)S(1)} %copy-done, f32[1,128]{1,0:T(1,128)S(1)} %bitcast.1), custom_call_target="tpu_custom_call" | custom-call | flops 2147483648 | bytes 8388608 | tf_op jit(solution)/shard_map/pallas_call | solution.py:282
  69.4 0.7 copy.5
Async XLA Ops:
  0.0 0.9 %copy-start = (bf16[16,4096]{1,0:T(8,128)(2,1)S(1)}, bf16[16,4096]{1,0:T(8,128)(2,1)}, u32[]{:S(2)}) copy-start(bf16[16,4096]{1,0:T(8,128)(2,1)} %target.1) | copy-start | bytes 393220
  0.9 0.7 copy-start.1

commit v3 on v2

--- a/solution.py
+++ b/solution.py
@@ -9,6 +9,7 @@
 from jax.sharding import PartitionSpec as P
 
 ITERS = 3
+DIRECT = 64
 MESH = pl.DeviceIdType.MESH
 
 
@@ -18,7 +19,7 @@
         dst_ref=dst,
         send_sem=send,
         recv_sem=recv,
-        device_id={axis: peer},
+        device_id=peer if axis is None else {axis: peer},
         device_id_type=MESH,
     )
 
@@ -26,7 +27,7 @@
 def kernel(
     n, nf, chunks,
     train_hbm, target, mass_hbm, out,
-    train, tg, part, rs, plan_t, macc, mb, xr, cb, mr, mass_row, mass_col,
+    train, tg, part, rs, scores, expo, plan_t, macc, mb, xr, cb, mr, mass_row, mass_col,
     ft_send, ft_recv, ex_send, ex_recv,
     load_sem, own_sem, mass_sem, g_send, g_recv, f_send, f_recv, r_send, r_recv,
     t_send, t_recv, s_send, s_recv, a_send, a_recv, x_send, x_recv, m_send, m_recv,
@@ -63,6 +64,16 @@
     def span(c):
         return pl.ds(c * dc, dc)
 
+    direct = n * nf <= DIRECT
+    place = me * nf + mf
+    ex_peers = [{"ex": ex_at(k)} for k in range(1, n)]
+    feat_peers = [{"feat": feat_at(k)} for k in range(1, nf)]
+    all_peers = []
+    if direct:
+        for k in range(1, n * nf):
+            index = lax.rem(place + k, n * nf)
+            all_peers.append({"ex": index // nf, "feat": lax.rem(index, nf)})
+
     mass_load = pltpu.make_async_copy(mass_hbm, mass_row, mass_sem)
     mass_load.start()
     own_load = pltpu.make_async_copy(target, tg.at[block(me, t)], own_sem)
@@ -75,11 +86,10 @@
         loads[-1].start()
 
     barrier = pltpu.get_barrier_semaphore()
-    for k in range(1, n):
-        pl.semaphore_signal(barrier, inc=1, device_id={"ex": ex_at(k)}, device_id_type=MESH)
-    for k in range(1, nf):
-        pl.semaphore_signal(barrier, inc=1, device_id={"feat": feat_at(k)}, device_id_type=MESH)
-    pl.semaphore_wait(barrier, n + nf - 2)
+    greeted = all_peers if direct else ex_peers + feat_peers
+    for peer in greeted:
+        pl.semaphore_signal(barrier, inc=1, device_id=peer, device_id_type=MESH)
+    pl.semaphore_wait(barrier, len(greeted))
 
     gathers = []
     forwards = []
@@ -156,20 +166,32 @@
     for k in range(1, nf):
         logits = logits + rs[k]
     logits = logits * scale
-    part[block(mf, rf), :] = logits
-
-    def exchange(step, axis, send, recv, here, at, size, send_sem, recv_sem, top, total):
+    scores[block(mf, rf), :] = logits
+    spreads = []
+    for k in range(1, nf):
+        copy = remote(
+            scores.at[block(mf, rf)], scores.at[block(mf, rf)],
+            a_send.at[k], a_recv.at[k], "feat", feat_at(k),
+        )
+        spreads.append(copy)
+
+    def row_lse(value):
+        top = jnp.max(value, axis=1, keepdims=True)
+        return top + jnp.log(jnp.sum(jnp.exp(value - top), axis=1, keepdims=True))
+
+    def exchange(step, send, recv, here, peers, send_sem, recv_sem, top, total, beside):
         send[step, 0:1, :] = top
         send[step, 1:2, :] = total
         wave = []
-        for k in range(1, size):
+        for k, peer in enumerate(peers):
             copy = remote(
                 send.at[step], recv.at[step, here],
-                send_sem.at[step, k], recv_sem.at[step, k], axis, at(k),
+                send_sem.at[step, k], recv_sem.at[step, k], None, peer,
             )
             copy.start()
             wave.append(copy)
         recv[step, here] = send[step]
+        beside()
         for copy in wave:
             copy.wait_recv()
         tops = recv[step, :, 0, :]
@@ -179,34 +201,40 @@
 
     col_pot = jnp.zeros((1, nt), jnp.float32)
     stats = []
-    row_pot = None
     for step in range(ITERS):
-        value = logits + col_pot
-        top = jnp.max(value, axis=1, keepdims=True)
-        row_pot = log_a - (top + jnp.log(jnp.sum(jnp.exp(value - top), axis=1, keepdims=True)))
+        row_pot = log_a - row_lse(logits + col_pot)
         value = logits + row_pot
         top = jnp.max(value, axis=0, keepdims=True)
         total = jnp.sum(jnp.exp(value - top), axis=0, keepdims=True)
+
+        def beside(step=step, col_pot=col_pot):
+            if step == 0:
+                for copy in spreads:
+                    copy.start()
+            if step == ITERS - 1:
+                for copy in spreads:
+                    copy.wait_recv()
+
+                @pl.loop(0, nf)
+                def _(index):
+                    full = scores[block(index, rf), :]
+                    expo[block(index, rf), :] = full + (log_a - row_lse(full + col_pot))
+
+        if not direct:
+            top, total, wave = exchange(
+                step, ft_send, ft_recv, mf, feat_peers, t_send, t_recv, top, total, lambda: None
+            )
+            stats += wave
         top, total, wave = exchange(
-            step, "feat", ft_send, ft_recv, mf, feat_at, nf, t_send, t_recv, top, total
-        )
-        stats += wave
-        top, total, wave = exchange(
-            step, "ex", ex_send, ex_recv, me, ex_at, n, s_send, s_recv, top, total
+            step, ex_send, ex_recv, place if direct else me,
+            all_peers if direct else ex_peers, s_send, s_recv, top, total, beside,
         )
         stats += wave
         col_pot = log_b - (top + jnp.log(total))
 
-    plan_t[mf] = jnp.exp(logits + row_pot + col_pot).T.astype(jnp.bfloat16)
-    spreads = []
-    for k in range(1, nf):
-        copy = remote(
-            plan_t.at[mf], plan_t.at[mf], a_send.at[k], a_recv.at[k], "feat", feat_at(k)
-        )
-        copy.start()
-        spreads.append(copy)
-    for copy in spreads:
-        copy.wait_recv()
+    for f in range(nf):
+        here = slice(f * rf, (f + 1) * rf)
+        plan_t[:, here] = jnp.exp(expo[here, :] + col_pot).T.astype(jnp.bfloat16)
 
     tile = math.gcd(dc, 256)
     swaps = []
@@ -216,12 +244,7 @@
         @pl.loop(0, dc // tile)
         def _(index):
             where = pl.ds(pl.multiple_of(c * dc + index * tile, tile), tile)
-            value = jnp.zeros((nt, tile), jnp.float32)
-            for f in range(nf):
-                value += jnp.dot(
-                    plan_t[f], train[f * rf:(f + 1) * rf, where],
-                    preferred_element_type=jnp.float32,
-                )
+            value = jnp.dot(plan_t[...], train[:, where], preferred_element_type=jnp.float32)
             value = value.reshape(nq, 2, t, tile)
             macc[:, :, :, where] = value
             mb[:, :, :, where] = value.astype(jnp.bfloat16)
@@ -274,6 +297,7 @@
     t = target_grads.shape[0]
     nt = t * n
     nq = n // 2
+    group = n * nf if n * nf <= DIRECT else n
     chunks = 4 if depth % 512 == 0 else 1
     f32, bf16 = jnp.float32, jnp.bfloat16
     vmem = pl.BlockSpec(memory_space=pltpu.VMEM)
@@ -289,7 +313,9 @@
             pltpu.VMEM((nt, depth), bf16),
             pltpu.VMEM((rows, nt), f32),
             pltpu.VMEM((nf, rows // nf, nt), f32),
-            pltpu.VMEM((nf, nt, rows // nf), bf16),
+            pltpu.VMEM((rows, nt), f32),
+            pltpu.VMEM((rows, nt), f32),
+            pltpu.VMEM((nt, rows), bf16),
             pltpu.VMEM((nq, 2, t, depth), f32),
             pltpu.VMEM((nq, 2, t, depth), bf16),
             pltpu.VMEM((nq, t, depth), bf16),
@@ -297,16 +323,16 @@
             pltpu.VMEM((nq, t, depth), bf16),
             pltpu.VMEM((1, nt), f32),
             pltpu.VMEM((nt, 8), f32),
-            pltpu.VMEM((ITERS, 8, nt), f32),
-            pltpu.VMEM((ITERS, nf, 8, nt), f32),
-            pltpu.VMEM((ITERS, 8, nt), f32),
-            pltpu.VMEM((ITERS, n, 8, nt), f32),
+            pltpu.VMEM((ITERS, 2, nt), f32),
+            pltpu.VMEM((ITERS, nf, 2, nt), f32),
+            pltpu.VMEM((ITERS, 2, nt), f32),
+            pltpu.VMEM((ITERS, group, 2, nt), f32),
             dma((chunks,)), dma, dma,
             dma((chunks, nq)), dma((chunks, nq)),
             dma((chunks, nq)), dma((chunks, nq)),
             dma((nf,)), dma((nf,)),
             dma((ITERS, nf)), dma((ITERS, nf)),
-            dma((ITERS, n)), dma((ITERS, n)),
+            dma((ITERS, group)), dma((ITERS, group)),
             dma((nf,)), dma((nf,)),
             dma((chunks,)), dma((chunks,)),
             dma((chunks, nq)), dma((chunks, nq)),

time: 70.2 us -> 65.7 us (0.936)
  Pallas kernels: 67.8 us -> 63.3 us
    pallas_call x1, Pallas kernels: 67.8 us -> 63.3 us  [shards(): pl.pallas_call(functools.partial(kernel, n, nf, chunks), out_shape=jax.Sh...]
where the time goes in v3:
time: 65.7 us; the launch traced here: 65.5 us
  Pallas kernels  63.3 us (96%)
  local copies, waits for them, and re-layouts  2.22 us (3%)
    pallas_call x1, Pallas kernels, shards(): pl.pallas_call(functools.partial(kernel, n, nf, chunks), out_shape=jax.Sh...  63.3 us
    unnamed x5, local copies, waits for them, and re-layouts  2.22 us

profile of v3, /device:TPU:0, one launch (start us, length us, event | category | flops | bytes accessed | tf_op | source)
XLA Modules:
  0.0 65.5 jit_solution(9110023615872135207)
XLA Ops:
  0.0 0.0 copy-start
  0.0 0.9 %copy-done = bf16[16,4096]{1,0:T(8,128)(2,1)S(1)} copy-done((bf16[16,4096]{1,0:T(8,128)(2,1)S(1)}, bf16[16,4096]{1,0:T(8,128)(2,1)}, u32[]{:S(2)}) %copy-start) | copy-done | bytes 131096
  0.9 0.0 copy-start.1
  0.9 0.7 copy-done.1
  1.6 63.3 %shard_map.37 = bf16[16,4096]{1,0:T(8,128)(2,1)S(1)} custom-call(bf16[1024,4096]{1,0:T(8,128)(2,1)} %train_hbm.1, bf16[16,4096]{1,0:T(8,128)(2,1)S(1)} %copy-done, f32[1,128]{1,0:T(1,128)S(1)} %bitcast.1), custom_call_target="tpu_custom_call" | custom-call | flops 2147483648 | bytes 8388608 | tf_op jit(solution)/shard_map/pallas_call | solution.py:306
  64.9 0.7 %copy.5 = bf16[16,4096]{1,0:T(8,128)(2,1)} copy(bf16[16,4096]{1,0:T(8,128)(2,1)S(1)} %shard_map.37) | data formatting | bytes 262144
Async XLA Ops:
  0.0 0.9 %copy-start = (bf16[16,4096]{1,0:T(8,128)(2,1)S(1)}, bf16[16,4096]{1,0:T(8,128)(2,1)}, u32[]{:S(2)}) copy-start(bf16[16,4096]{1,0:T(8,128)(2,1)} %target.1) | copy-start | bytes 393220
  0.9 0.7 copy-start.1

commit v4 on v3

--- a/solution.py
+++ b/solution.py
@@ -9,7 +9,6 @@
 from jax.sharding import PartitionSpec as P
 
 ITERS = 3
-DIRECT = 64
 MESH = pl.DeviceIdType.MESH
 
 
@@ -27,7 +26,7 @@
 def kernel(
     n, nf, chunks,
     train_hbm, target, mass_hbm, out,
-    train, tg, part, rs, scores, expo, plan_t, macc, mb, xr, cb, mr, mass_row, mass_col,
+    train, tg, part, rs, scores, plan_t, macc, mb, xr, cb, mr, mass_row, mass_col,
     ft_send, ft_recv, ex_send, ex_recv,
     load_sem, own_sem, mass_sem, g_send, g_recv, f_send, f_recv, r_send, r_recv,
     t_send, t_recv, s_send, s_recv, a_send, a_recv, x_send, x_recv, m_send, m_recv,
@@ -64,15 +63,8 @@
     def span(c):
         return pl.ds(c * dc, dc)
 
-    direct = n * nf <= DIRECT
-    place = me * nf + mf
     ex_peers = [{"ex": ex_at(k)} for k in range(1, n)]
     feat_peers = [{"feat": feat_at(k)} for k in range(1, nf)]
-    all_peers = []
-    if direct:
-        for k in range(1, n * nf):
-            index = lax.rem(place + k, n * nf)
-            all_peers.append({"ex": index // nf, "feat": lax.rem(index, nf)})
 
     mass_load = pltpu.make_async_copy(mass_hbm, mass_row, mass_sem)
     mass_load.start()
@@ -86,7 +78,7 @@
         loads[-1].start()
 
     barrier = pltpu.get_barrier_semaphore()
-    greeted = all_peers if direct else ex_peers + feat_peers
+    greeted = ex_peers + feat_peers
     for peer in greeted:
         pl.semaphore_signal(barrier, inc=1, device_id=peer, device_id_type=MESH)
     pl.semaphore_wait(barrier, len(greeted))
@@ -199,42 +191,34 @@
         total = jnp.sum(recv[step, :, 1, :] * jnp.exp(tops - top), axis=0, keepdims=True)
         return top, total, wave
 
+    def spread():
+        for copy in spreads:
+            copy.start()
+
     col_pot = jnp.zeros((1, nt), jnp.float32)
     stats = []
     for step in range(ITERS):
-        row_pot = log_a - row_lse(logits + col_pot)
-        value = logits + row_pot
+        if step == 1:
+            for copy in spreads:
+                copy.wait_recv()
+        known = logits if step == 0 else scores[...]
+        row_pot = log_a - row_lse(known + col_pot)
+        value = known + row_pot
         top = jnp.max(value, axis=0, keepdims=True)
         total = jnp.sum(jnp.exp(value - top), axis=0, keepdims=True)
-
-        def beside(step=step, col_pot=col_pot):
-            if step == 0:
-                for copy in spreads:
-                    copy.start()
-            if step == ITERS - 1:
-                for copy in spreads:
-                    copy.wait_recv()
-
-                @pl.loop(0, nf)
-                def _(index):
-                    full = scores[block(index, rf), :]
-                    expo[block(index, rf), :] = full + (log_a - row_lse(full + col_pot))
-
-        if not direct:
+        if step == 0:
             top, total, wave = exchange(
-                step, ft_send, ft_recv, mf, feat_peers, t_send, t_recv, top, total, lambda: None
+                step, ft_send, ft_recv, mf, feat_peers, t_send, t_recv, top, total, spread
             )
             stats += wave
         top, total, wave = exchange(
-            step, ex_send, ex_recv, place if direct else me,
-            all_peers if direct else ex_peers, s_send, s_recv, top, total, beside,
+            step, ex_send, ex_recv, me, ex_peers, s_send, s_recv, top, total, lambda: None
         )
         stats += wave
         col_pot = log_b - (top + jnp.log(total))
 
-    for f in range(nf):
-        here = slice(f * rf, (f + 1) * rf)
-        plan_t[:, here] = jnp.exp(expo[here, :] + col_pot).T.astype(jnp.bfloat16)
+    plan = jnp.exp(scores[...] + row_pot + col_pot)
+    plan_t[...] = plan.T.astype(jnp.bfloat16)
 
     tile = math.gcd(dc, 256)
     swaps = []
@@ -297,7 +281,6 @@
     t = target_grads.shape[0]
     nt = t * n
     nq = n // 2
-    group = n * nf if n * nf <= DIRECT else n
     chunks = 4 if depth % 512 == 0 else 1
     f32, bf16 = jnp.float32, jnp.bfloat16
     vmem = pl.BlockSpec(memory_space=pltpu.VMEM)
@@ -314,7 +297,6 @@
             pltpu.VMEM((rows, nt), f32),
             pltpu.VMEM((nf, rows // nf, nt), f32),
             pltpu.VMEM((rows, nt), f32),
-            pltpu.VMEM((rows, nt), f32),
             pltpu.VMEM((nt, rows), bf16),
             pltpu.VMEM((nq, 2, t, depth), f32),
             pltpu.VMEM((nq, 2, t, depth), bf16),
@@ -326,13 +308,13 @@
             pltpu.VMEM((ITERS, 2, nt), f32),
             pltpu.VMEM((ITERS, nf, 2, nt), f32),
             pltpu.VMEM((ITERS, 2, nt), f32),
-            pltpu.VMEM((ITERS, group, 2, nt), f32),
+            pltpu.VMEM((ITERS, n, 2, nt), f32),
             dma((chunks,)), dma, dma,
             dma((chunks, nq)), dma((chunks, nq)),
             dma((chunks, nq)), dma((chunks, nq)),
             dma((nf,)), dma((nf,)),
             dma((ITERS, nf)), dma((ITERS, nf)),
-            dma((ITERS, group)), dma((ITERS, group)),
+            dma((ITERS, n)), dma((ITERS, n)),
             dma((nf,)), dma((nf,)),
             dma((chunks,)), dma((chunks,)),
             dma((chunks, nq)), dma((chunks, nq)),

time: 65.7 us -> 59.9 us (0.912)
  Pallas kernels: 63.3 us -> 57.2 us
    pallas_call x1, Pallas kernels: 63.3 us -> 57.2 us  [shards(): pl.pallas_call(functools.partial(kernel, n, nf, chunks), out_shape=jax.Sh...]
where the time goes in v4:
time: 59.9 us; the launch traced here: 59.5 us
  Pallas kernels  57.2 us (95%)
  local copies, waits for them, and re-layouts  2.22 us (4%)
    pallas_call x1, Pallas kernels, shards(): pl.pallas_call(functools.partial(kernel, n, nf, chunks), out_shape=jax.Sh...  57.2 us
    unnamed x5, local copies, waits for them, and re-layouts  2.22 us

profile of v4, /device:TPU:0, one launch (start us, length us, event | category | flops | bytes accessed | tf_op | source)
XLA Modules:
  0.0 59.5 jit_solution(4594092900187117360)
XLA Ops:
  0.0 0.0 copy-start
  0.0 0.9 %copy-done = bf16[16,4096]{1,0:T(8,128)(2,1)S(1)} copy-done((bf16[16,4096]{1,0:T(8,128)(2,1)S(1)}, bf16[16,4096]{1,0:T(8,128)(2,1)}, u32[]{:S(2)}) %copy-start) | copy-done | bytes 131096
  0.9 0.0 copy-start.1
  0.9 0.7 %copy-done.1 = f32[128]{0:T(128)S(1)} copy-done((f32[128]{0:T(128)S(1)}, f32[128]{0:T(128)}, u32[]{:S(2)}) %copy-start.1) | copy-done | bytes 536
  1.6 57.2 %shard_map.37 = bf16[16,4096]{1,0:T(8,128)(2,1)S(1)} custom-call(bf16[1024,4096]{1,0:T(8,128)(2,1)} %train_hbm.1, bf16[16,4096]{1,0:T(8,128)(2,1)S(1)} %copy-done, f32[1,128]{1,0:T(1,128)S(1)} %bitcast.1), custom_call_target="tpu_custom_call" | custom-call | flops 2147483648 | bytes 8388608 | tf_op jit(solution)/shard_map/pallas_call | solution.py:289
  58.8 0.7 %copy.5 = bf16[16,4096]{1,0:T(8,128)(2,1)} copy(bf16[16,4096]{1,0:T(8,128)(2,1)S(1)} %shard_map.37) | data formatting | bytes 262144
Async XLA Ops:
  0.0 0.9 %copy-start = (bf16[16,4096]{1,0:T(8,128)(2,1)S(1)}, bf16[16,4096]{1,0:T(8,128)(2,1)}, u32[]{:S(2)}) copy-start(bf16[16,4096]{1,0:T(8,128)(2,1)} %target.1) | copy-start | bytes 393220
  0.9 0.7 %copy-start.1 = (f32[128]{0:T(128)S(1)}, f32[128]{0:T(128)}, u32[]{:S(2)}) copy-start(f32[128]{0:T(128)} %param.5) | copy-start | bytes 1540

commit v5 on v4

--- a/solution.py
+++ b/solution.py
@@ -165,13 +165,14 @@
             scores.at[block(mf, rf)], scores.at[block(mf, rf)],
             a_send.at[k], a_recv.at[k], "feat", feat_at(k),
         )
+        copy.start()
         spreads.append(copy)
 
     def row_lse(value):
         top = jnp.max(value, axis=1, keepdims=True)
         return top + jnp.log(jnp.sum(jnp.exp(value - top), axis=1, keepdims=True))
 
-    def exchange(step, send, recv, here, peers, send_sem, recv_sem, top, total, beside):
+    def exchange(step, send, recv, here, peers, send_sem, recv_sem, top, total):
         send[step, 0:1, :] = top
         send[step, 1:2, :] = total
         wave = []
@@ -183,17 +184,12 @@
             copy.start()
             wave.append(copy)
         recv[step, here] = send[step]
-        beside()
         for copy in wave:
             copy.wait_recv()
         tops = recv[step, :, 0, :]
         top = jnp.max(tops, axis=0, keepdims=True)
         total = jnp.sum(recv[step, :, 1, :] * jnp.exp(tops - top), axis=0, keepdims=True)
         return top, total, wave
-
-    def spread():
-        for copy in spreads:
-            copy.start()
 
     col_pot = jnp.zeros((1, nt), jnp.float32)
     stats = []
@@ -208,11 +204,11 @@
         total = jnp.sum(jnp.exp(value - top), axis=0, keepdims=True)
         if step == 0:
             top, total, wave = exchange(
-                step, ft_send, ft_recv, mf, feat_peers, t_send, t_recv, top, total, spread
+                step, ft_send, ft_recv, mf, feat_peers, t_send, t_recv, top, total
             )
             stats += wave
         top, total, wave = exchange(
-            step, ex_send, ex_recv, me, ex_peers, s_send, s_recv, top, total, lambda: None
+            step, ex_send, ex_recv, me, ex_peers, s_send, s_recv, top, total
         )
         stats += wave
         col_pot = log_b - (top + jnp.log(total))

time: 59.9 us -> 64.6 us (1.078)
  Pallas kernels: 57.2 us -> 62.2 us
    pallas_call x1, Pallas kernels: 57.2 us -> 62.2 us  [shards(): pl.pallas_call(functools.partial(kernel, n, nf, chunks), out_shape=jax.Sh...]
where the time goes in v5:
time: 64.6 us; the launch traced here: 64.4 us
  Pallas kernels  62.2 us (96%)
  local copies, waits for them, and re-layouts  2.22 us (3%)
    pallas_call x1, Pallas kernels, shards(): pl.pallas_call(functools.partial(kernel, n, nf, chunks), out_shape=jax.Sh...  62.2 us
    unnamed x5, local copies, waits for them, and re-layouts  2.22 us

profile of v5, /device:TPU:0, one launch (start us, length us, event | category | flops | bytes accessed | tf_op | source)
XLA Modules:
  0.0 64.4 jit_solution(10178584308345997472)
XLA Ops:
  0.0 0.0 copy-start
  0.0 0.9 %copy-done = bf16[16,4096]{1,0:T(8,128)(2,1)S(1)} copy-done((bf16[16,4096]{1,0:T(8,128)(2,1)S(1)}, bf16[16,4096]{1,0:T(8,128)(2,1)}, u32[]{:S(2)}) %copy-start) | copy-done | bytes 131096
  0.9 0.0 copy-start.1
  0.9 0.7 %copy-done.1 = f32[128]{0:T(128)S(1)} copy-done((f32[128]{0:T(128)S(1)}, f32[128]{0:T(128)}, u32[]{:S(2)}) %copy-start.1) | copy-done | bytes 536
  1.6 62.2 %shard_map.37 = bf16[16,4096]{1,0:T(8,128)(2,1)S(1)} custom-call(bf16[1024,4096]{1,0:T(8,128)(2,1)} %train_hbm.1, bf16[16,4096]{1,0:T(8,128)(2,1)S(1)} %copy-done, f32[1,128]{1,0:T(1,128)S(1)} %bitcast.1), custom_call_target="tpu_custom_call" | custom-call | flops 2147483648 | bytes 8388608 | tf_op jit(solution)/shard_map/pallas_call | solution.py:285
  63.8 0.7 %copy.5 = bf16[16,4096]{1,0:T(8,128)(2,1)} copy(bf16[16,4096]{1,0:T(8,128)(2,1)S(1)} %shard_map.37) | data formatting | bytes 262144
Async XLA Ops:
  0.0 0.9 %copy-start = (bf16[16,4096]{1,0:T(8,128)(2,1)S(1)}, bf16[16,4096]{1,0:T(8,128)(2,1)}, u32[]{:S(2)}) copy-start(bf16[16,4096]{1,0:T(8,128)(2,1)} %target.1) | copy-start | bytes 393220
  0.9 0.7 %copy-start.1 = (f32[128]{0:T(128)S(1)}, f32[128]{0:T(128)}, u32[]{:S(2)}) copy-start(f32[128]{0:T(128)} %param.5) | copy-start | bytes 1540
